TPU v7x, 128 devices: a whole 4x4x4 slice. The times are simulated.
128 devices in a mesh: pipe: 4 (over y), dp: 32 (over z, x, core).
Axes of the slice: x: 4, y: 4, z: 4, core: 2. Of those that a mesh axis runs over, the one named last changes fastest.
Arguments:
- cotangent: bfloat16 [2, 128, 4096], P(None, None, 'dp'), may hold values from -4 to 4
- stashed_inputs: bfloat16 [4, 2, 128, 4096], P('pipe', None, None, 'dp'), may hold values from -4 to 4
- weights: bfloat16 [4, 4096, 4096], P('pipe', 'dp'), may hold values from -0.09375 to 0.09375
- momentum: bfloat16 [4, 4096, 4096], P('pipe', 'dp'), may hold values from -560 to 560
Outputs:
- input_grads: bfloat16 [4, 2, 128, 4096], P('pipe', None, None, 'dp')
- new_momentum: bfloat16 [4, 4096, 4096], P('pipe', 'dp')
- orth_update: bfloat16 [4, 4096, 4096], P('pipe', 'dp')
All inputs are finite; a program needn't handle non-finite values.
Results may differ from a plain program's by a relative error of at most 0.008.
Values may be sent and summed in bfloat16 or wider, within the bound.
A program may use at most 192 MiB of HBM per device.

v0:
```python
import math
import jax
import jax.numpy as jnp
from jax import lax
from jax.sharding import PartitionSpec as P

quintic_a = 3.4445
quintic_b = -4.775
quintic_c = 2.0315


def from_behind(value, axis, steps):
    count = lax.axis_size(axis)
    leading, last = (max(0, -steps), min(count, count - steps))
    return lax.ppermute(value, axis, [(source, source + steps) for source in range(leading, last)])


def contract_last(left_part, right_part):
    return lax.dot_general(
        left_part, right_part, (((1,), (1,)), ((), ())), preferred_element_type=jnp.float32
    )


def per_device(cotangent, stashed_inputs, weights, momentum):
    layers = lax.axis_size("pipe")
    section = lax.axis_index("pipe")
    micro_count = cotangent.shape[0]
    tok_rows = cotangent.shape[1]
    width_loc = cotangent.shape[2]
    weight_rows = weights[0]
    width_full = weight_rows.shape[1]
    activations = stashed_inputs[0].astype(jnp.float32)
    sigmoid_val = jax.nn.sigmoid(activations)
    slopes = sigmoid_val * (1.0 + activations * (1.0 - sigmoid_val))
    gated_acts = (activations * sigmoid_val).astype(jnp.bfloat16)
    incoming = jnp.zeros((tok_rows, width_loc), jnp.bfloat16)
    out_grads = jnp.zeros((micro_count, tok_rows, width_loc), jnp.bfloat16)
    weight_grad = jnp.zeros((width_loc, width_full), jnp.float32)
    steps_all = micro_count + layers - 1
    for step_index in range(steps_all):
        micro_index = step_index - (layers - 1 - section)
        is_valid = (micro_index >= 0) & (micro_index < micro_count)
        slot_index = jnp.clip(micro_index, 0, micro_count - 1)
        own_grad = lax.dynamic_index_in_dim(cotangent, slot_index, 0, keepdims=False)
        upstream = jnp.where(section == layers - 1, own_grad, incoming)
        full_grad = lax.all_gather(upstream, "dp", axis=1, tiled=True)
        back_proj = contract_last(full_grad, weight_rows)
        slope_now = lax.dynamic_index_in_dim(slopes, slot_index, 0, keepdims=False)
        dinput = (upstream.astype(jnp.float32) + slope_now * back_proj).astype(jnp.bfloat16)
        out_grads = jnp.where(
            is_valid, lax.dynamic_update_index_in_dim(out_grads, dinput, slot_index, 0), out_grads
        )
        gated_now = lax.dynamic_index_in_dim(gated_acts, slot_index, 0, keepdims=False)
        weight_term = lax.dot_general(
            gated_now, full_grad, (((0,), (0,)), ((), ())), preferred_element_type=jnp.float32
        )
        weight_grad = weight_grad + jnp.where(is_valid, weight_term, 0.0)
        if step_index + 1 < steps_all:
            incoming = from_behind(dinput, "pipe", -1)
    entries = float(width_full) * float(width_full)
    fresh_moment = (0.95 * momentum[0].astype(jnp.float32) + weight_grad).astype(jnp.bfloat16)
    fresh32 = fresh_moment.astype(jnp.float32)
    sum_squares = lax.psum(jnp.sum(fresh32 * fresh32), "dp")
    scaling = 0.4 / jnp.sqrt(width_full * (sum_squares / entries + 1e-06))
    scaled_rows = (fresh32 * scaling).astype(jnp.bfloat16)
    whole_matrix = lax.all_gather(scaled_rows, "dp", axis=0, tiled=True)
    gram_rows = contract_last(scaled_rows, whole_matrix).astype(jnp.bfloat16)
    cubic_rows = jnp.dot(gram_rows, whole_matrix, preferred_element_type=jnp.float32).astype(
        jnp.bfloat16
    )
    back_rows = contract_last(cubic_rows, whole_matrix).astype(jnp.bfloat16)
    quintic_rows = jnp.dot(back_rows, whole_matrix, preferred_element_type=jnp.float32)
    mixed = (
        quintic_a * scaled_rows.astype(jnp.float32)
        + quintic_b * cubic_rows.astype(jnp.float32)
        + quintic_c * quintic_rows
    )
    update_rows = (math.sqrt(width_full) * mixed).astype(jnp.bfloat16)
    return (out_grads[None], fresh_moment[None], update_rows[None])


def solution(mesh):
    in_specs = (
        P(None, None, "dp"),
        P("pipe", None, None, "dp"),
        P("pipe", "dp", None),
        P("pipe", "dp", None),
    )
    out_specs = (P("pipe", None, None, "dp"), P("pipe", "dp", None), P("pipe", "dp", None))
    return jax.shard_map(
        per_device, mesh=mesh, in_specs=in_specs, out_specs=out_specs, check_vma=False
    )
```

profile of v0, /device:TPU:1, one launch (start us, length us, event | category | flops | bytes accessed | tf_op | source)
XLA Modules:
  0.0 517.5 jit_solution(9246325424143566442)
XLA Ops:
  7.2 1.5 dynamic-slice_select_fusion
  9.7 47.8 %all-gather.18.cloned.1.call-done = bf16[1,128,4096]{2,1,0:T(8,128)(2,1)} async-done(((bf16[1,128,128]{2,1,0:T(8,128)(2,1)}), bf16[1,128,4096]{2,1,0:T(8,128)(2,1)}) %all-gather.18.cloned.1.call-update) | async-done | bytes 1048592 | tf_op jit(solution)/shard_map/all_gather | solution.py:46
  57.6 1.7 bitcast_dynamic-update-slice_fusion
  60.6 3.4 collective-permute-done
  64.6 43.6 %all-gather.8.cloned.1.call-done = bf16[128,4096]{1,0:T(8,128)(2,1)} async-done(((bf16[128,128]{1,0:T(8,128)(2,1)}), bf16[128,4096]{1,0:T(8,128)(2,1)}) %all-gather.8.cloned.1.call-update) | async-done | bytes 1048592 | tf_op jit(solution)/shard_map/all_gather | solution.py:46
  108.2 1.7 fusion.38
  111.2 3.4 collective-permute-done.1
  115.3 43.6 %all-gather.10.cloned.1.call-done = bf16[128,4096]{1,0:T(8,128)(2,1)} async-done(((bf16[128,128]{1,0:T(8,128)(2,1)}), bf16[128,4096]{1,0:T(8,128)(2,1)}) %all-gather.10.cloned.1.call-update) | async-done | bytes 1048592 | tf_op jit(solution)/shard_map/all_gather | solution.py:46
  158.9 1.7 fusion.37
  161.9 3.4 collective-permute-done.2
  166.0 43.6 %all-gather.12.cloned.1.call-done = bf16[128,4096]{1,0:T(8,128)(2,1)} async-done(((bf16[128,128]{1,0:T(8,128)(2,1)}), bf16[128,4096]{1,0:T(8,128)(2,1)}) %all-gather.12.cloned.1.call-update) | async-done | bytes 1048592 | tf_op jit(solution)/shard_map/all_gather | solution.py:46
  209.6 1.7 fusion.36
  212.6 3.4 collective-permute-done.3
  216.6 1.7 convolution_select_fusion.4
  218.3 3.1 convolution_select_fusion.2
  221.5 1.8 convolution_select_fusion.1
  223.2 37.0 %all-gather.14.cloned.1.call-done = bf16[128,4096]{1,0:T(8,128)(2,1)} async-done(((bf16[128,128]{1,0:T(8,128)(2,1)}), bf16[128,4096]{1,0:T(8,128)(2,1)}) %all-gather.14.cloned.1.call-update) | async-done | bytes 1048592 | tf_op jit(solution)/shard_map/all_gather | solution.py:46
  260.3 1.8 convolution_select_fusion
  262.4 4.6 fusion.10
  267.0 63.1 %psum.7 = f32[]{:T(128)} all-reduce(f32[]{:T(128)} %get-tuple-element.13), channel_id=1, replica_groups=mesh['pipe'=4,'dp'=32] {'dp'}, use_global_device_ids=true, to_apply=%region_1.2 | all-reduce | flops 1 | bytes 8 | tf_op jit(solution)/shard_map/psum | solution.py:63
  330.8 2.4 fusion.11
  333.7 112.8 %all-gather.16.cloned.1.call-done = bf16[4096,4096]{1,0:T(8,128)(2,1)} async-done(((bf16[128,4096]{1,0:T(8,128)(2,1)}), bf16[4096,4096]{1,0:T(8,128)(2,1)}) %all-gather.16.cloned.1.call-update) | async-done | bytes 33554448 | tf_op jit(solution)/shard_map/all_gather | solution.py:66
  446.5 31.3 %convolution_convert_fusion.1 = bf16[128,4096]{1,0:T(8,128)(2,1)S(1)} fusion(bf16[4096,4096]{1,0:T(8,128)(2,1)} %all-gather.16.cloned.1.call-done, bf16[128,4096]{1,0:T(8,128)(2,1)S(1)} %copy-done.1), kind=kOutput, calls=%fused_computation.15 | convolution fusion | flops 8590983168 | bytes 35651584 | tf_op jit(solution)/shard_map/dot_general | solution.py:68
  477.9 32.8 %fusion.9 = bf16[1,128,4096]{2,1,0:T(8,128)(2,1)} fusion(bf16[4096,4096]{1,0:T(8,128)(2,1)} %all-gather.16.cloned.1.call-done, bf16[128,4096]{1,0:T(8,128)(2,1)S(1)} %convolution_convert_fusion.1, bf16[128,4096]{1,0:T(8,128)(2,1)S(1)} %copy-done.1), kind=kOutput, calls=%fused_computation.18 | convolution fusion | flops 8595177472 | bytes 36700160 | tf_op jit(solution)/shard_map/dot_general | solution.py:72
  (42 shorter events, 9.8 us)
Async XLA Ops:
  7.2 50.4 %copy-start = (bf16[1,128,4096]{2,1,0:T(8,128)(2,1)S(1)}, bf16[1,128,4096]{2,1,0:T(8,128)(2,1)}, u32[]{:S(2)}) copy-start(bf16[1,128,4096]{2,1,0:T(8,128)(2,1)} %param.6) | copy-start | bytes 3145732
  7.2 56.7 %copy-start.6 = (bf16[2,128,128]{2,1,0:T(8,128)(2,1)S(1)}, bf16[2,128,128]{2,1,0:T(8,128)(2,1)}, u32[]{:S(2)}) copy-start(bf16[2,128,128]{2,1,0:T(8,128)(2,1)} %param.4) | copy-start | bytes 196612
  7.2 50.3 %all-gather.18.cloned.1.call-start = ((), (), s32[]{:S(2)}) async-start(), calls=%async_computation.5 | async-start | bytes 1081344 | tf_op jit(solution)/shard_map/all_gather | solution.py:46
  8.7 99.5 %all-gather.8.cloned.1.call-start = ((), (), s32[]{:S(2)}) async-start(), calls=%async_computation | async-start | bytes 1081344 | tf_op jit(solution)/shard_map/all_gather | solution.py:46
  59.2 4.7 collective-permute-start
  64.6 94.4 %all-gather.10.cloned.1.call-start = ((), (), s32[]{:S(2)}) async-start(), calls=%async_computation.1 | async-start | bytes 1081344 | tf_op jit(solution)/shard_map/all_gather | solution.py:46
  109.9 4.7 collective-permute-start.1
  115.2 94.4 %all-gather.12.cloned.1.call-start = ((), (), s32[]{:S(2)}) async-start(), calls=%async_computation.2 | async-start | bytes 1081344 | tf_op jit(solution)/shard_map/all_gather | solution.py:46
  160.6 4.7 collective-permute-start.2
  165.9 94.4 %all-gather.14.cloned.1.call-start = ((), (), s32[]{:S(2)}) async-start(), calls=%async_computation.3 | async-start | bytes 1081344 | tf_op jit(solution)/shard_map/all_gather | solution.py:46
  211.3 4.7 collective-permute-start.3
  216.6 229.9 %all-gather.16.cloned.1.call-start = ((), (), s32[]{:S(2)}) async-start(), calls=%async_computation.4 | async-start | bytes 34603008 | tf_op jit(solution)/shard_map/all_gather | solution.py:66
  218.3 3.1 copy-start.5
  260.3 1.9 copy-start.2
  260.3 2.2 copy-start.3
  267.0 66.2 %copy-start.4 = (bf16[128,4096]{1,0:T(8,128)(2,1)S(1)}, bf16[128,4096]{1,0:T(8,128)(2,1)}, u32[]{:S(2)}) copy-start(bf16[128,4096]{1,0:T(8,128)(2,1)} %all-gather.14.cloned.1.call-done) | copy-start | bytes 3145732
  267.0 66.2 %copy-start.7 = (bf16[128,128]{1,0:T(8,128)(2,1)S(1)}, bf16[128,128]{1,0:T(8,128)(2,1)}, u32[]{:S(2)}) copy-start(bf16[128,128]{1,0:T(8,128)(2,1)} %bitcast_select_fusion) | copy-start | bytes 98308
  333.2 113.3 %copy-start.1 = (bf16[128,4096]{1,0:T(8,128)(2,1)S(1)}, bf16[128,4096]{1,0:T(8,128)(2,1)}, u32[]{:S(2)}) copy-start(bf16[128,4096]{1,0:T(8,128)(2,1)} %fusion.11) | copy-start | bytes 3145732
  333.7 144.2 %copy-start.8 = (bf16[1,2,128,128]{3,2,1,0:T(8,128)(2,1)}, bf16[1,2,128,128]{3,2,1,0:T(8,128)(2,1)S(1)}, u32[]{:S(2)}) copy-start(bf16[1,2,128,128]{3,2,1,0:T(8,128)(2,1)S(1)} %fusion.30) | copy-start | bytes 196612
Sparse Core Ops, SparseCore 0:
  10.8 46.7 all-gather.17
  64.7 43.5 all-gather.7
  115.4 43.5 all-gather.9
  166.0 43.5 all-gather.11
  216.7 43.5 all-gather.13
  333.4 113.1 all-gather.15
where the time goes:
time: 518 us
  waiting for transfers between devices  342 us (66%)
  matrix products  84.3 us (16%)
  blocking collectives  63.1 us (12%)
  between operations  15 us (3%)
  other arithmetic  7.25 us (1%)
  starting transfers between devices  5.41 us (1%)
    all_gather x5, waiting for transfers between devices, per_device(): full_grad = lax.all_gather(upstream, 'dp', axis=1, tiled=True)  216 us
    all_gather x1, waiting for transfers between devices, per_device(): whole_matrix = lax.all_gather(scaled_rows, 'dp', axis=0, tiled=True)  113 us
    psum x1, blocking collectives, per_device(): sum_squares = lax.psum(jnp.sum(fresh32 * fresh32), 'dp')  63.1 us
    dot_general x1, matrix products, per_device(): jnp.dot(back_rows, whole_matrix, preferred_element_type=jnp.float32)  32.8 us
    dot_general x1, matrix products, per_device(): jnp.dot(gram_rows, whole_matrix, preferred_element_type=jnp.float32)  31.3 us
    ppermute x4, waiting for transfers between devices, from_behind(): lax.ppermute(value, axis, [(source, source + steps) for source in range(l...  13.4 us
    dot_general x5, matrix products, per_device(): lax.dot_general(gated_now, full_grad, (((0,), (0,)), ((), ())), preferred...  13 us
  transfers between devices with their start and end apart: 10, of which 10 were waited for; matrix products, arithmetic and copies ran while one was open for 2% of the time, Pallas kernels for 0%

commit v1 on v0

--- a/solution.py
+++ b/solution.py
@@ -7,6 +7,12 @@
 quintic_a = 3.4445
 quintic_b = -4.775
 quintic_c = 2.0315
+
+
+def gather_from_all(x, axis, dim):
+    length = lax.axis_size(axis)
+    repeats = [length if d == dim else 1 for d in range(x.ndim)]
+    return lax.all_to_all(jnp.tile(x, repeats), axis, split_axis=dim, concat_axis=dim, tiled=True)
 
 
 def from_behind(value, axis, steps):
@@ -43,7 +49,7 @@
         slot_index = jnp.clip(micro_index, 0, micro_count - 1)
         own_grad = lax.dynamic_index_in_dim(cotangent, slot_index, 0, keepdims=False)
         upstream = jnp.where(section == layers - 1, own_grad, incoming)
-        full_grad = lax.all_gather(upstream, "dp", axis=1, tiled=True)
+        full_grad = gather_from_all(upstream, "dp", 1)
         back_proj = contract_last(full_grad, weight_rows)
         slope_now = lax.dynamic_index_in_dim(slopes, slot_index, 0, keepdims=False)
         dinput = (upstream.astype(jnp.float32) + slope_now * back_proj).astype(jnp.bfloat16)

time: 518 us -> 426 us (0.82)
  waiting for transfers between devices: 342 us -> 207 us
  starting transfers between devices: 5.41 us -> 37.8 us
  local copies, waits for them, and re-layouts: 0.39 us -> 16 us
    all_gather x5 -> x0, waiting for transfers between devices: 216 us -> none  [per_device(): full_grad = lax.all_gather(upstream, 'dp', axis=1, tiled=True)]
    all_to_all x0 -> x5, waiting for transfers between devices: none -> 80.9 us  [gather_from_all(): lax.all_to_all(jnp.tile(x, repeats), axis, split_axis=dim, concat_axis=di...]
    all_to_all x0 -> x5, starting transfers between devices: none -> 32.6 us  [gather_from_all(): lax.all_to_all(jnp.tile(x, repeats), axis, split_axis=dim, concat_axis=di...]
    all_to_all x0 -> x5, local copies, waits for them, and re-layouts: none -> 8.41 us  [gather_from_all(): lax.all_to_all(jnp.tile(x, repeats), axis, split_axis=dim, concat_axis=di...]
    another operation x0 -> x5, local copies, waits for them, and re-layouts: none -> 6.15 us  [gather_from_all(): jnp.tile(x, repeats)]
  transfers between devices with their start and end apart: 10 -> 10, of which waited for: 10 -> 10; matrix products, arithmetic and copies ran while one was open for 2% -> 1% of each run, Pallas kernels for 0% -> 0%
where the time goes in v1:
time: 426 us; the launch traced here: 425 us
  waiting for transfers between devices  207 us (49%)
  matrix products  79.9 us (19%)
  blocking collectives  63.2 us (15%)
  starting transfers between devices  37.8 us (9%)
  local copies, waits for them, and re-layouts  16 us (4%)
  between operations  15 us (4%)
  other arithmetic  5.63 us (1%)
    all_gather x1, waiting for transfers between devices, per_device(): whole_matrix = lax.all_gather(scaled_rows, 'dp', axis=0, tiled=True)  112 us
    all_to_all x5, waiting for transfers between devices, gather_from_all(): lax.all_to_all(jnp.tile(x, repeats), axis, split_axis=dim, concat_axis=di...  80.9 us
    psum x1, blocking collectives, per_device(): sum_squares = lax.psum(jnp.sum(fresh32 * fresh32), 'dp')  63.2 us
    dot_general x1, matrix products, per_device(): jnp.dot(back_rows, whole_matrix, preferred_element_type=jnp.float32)  32.8 us
    all_to_all x5, starting transfers between devices, gather_from_all(): lax.all_to_all(jnp.tile(x, repeats), axis, split_axis=dim, concat_axis=di...  32.6 us
    dot_general x1, matrix products, per_device(): jnp.dot(gram_rows, whole_matrix, preferred_element_type=jnp.float32)  31.4 us
    ppermute x4, waiting for transfers between devices, from_behind(): lax.ppermute(value, axis, [(source, source + steps) for source in range(l...  13.7 us
    dot_general x5, matrix products, per_device(): lax.dot_general(gated_now, full_grad, (((0,), (0,)), ((), ())), preferred...  10.8 us
  transfers between devices with their start and end apart: 10, of which 10 were waited for; matrix products, arithmetic and copies ran while one was open for 1% of the time, Pallas kernels for 0%

profile of v1, /device:TPU:1, one launch (start us, length us, event | category | flops | bytes accessed | tf_op | source)
XLA Modules:
  0.0 424.6 jit_solution(10465964426487258318)
XLA Ops:
  9.3 9.4 %all-to-all-start = ((bf16[128,32,128]{2,0,1:T(8,128)(2,1)}), bf16[128,32,128]{2,0,1:T(8,128)(2,1)S(1)}, u32[]{:S(2)}, u32[]{:S(2)}) async-start(bf16[128,32,128]{2,0,1:T(8,128)(2,1)} %tile.10), calls=%async_computation | async-start | bytes 2097152 | tf_op jit(solution)/shard_map/all_to_all | solution.py:15
  18.8 17.1 %all-to-all-done = bf16[128,32,128]{2,0,1:T(8,128)(2,1)S(1)} async-done(((bf16[128,32,128]{2,0,1:T(8,128)(2,1)}), bf16[128,32,128]{2,0,1:T(8,128)(2,1)S(1)}, u32[]{:S(2)}, u32[]{:S(2)}) %all-to-all-start) | async-done | bytes 1048608 | tf_op jit(solution)/shard_map/all_to_all | solution.py:15
  38.4 3.4 collective-permute-done
  43.0 5.8 %all-to-all-start.1 = ((bf16[128,32,128]{2,0,1:T(8,128)(2,1)}), bf16[128,32,128]{2,0,1:T(8,128)(2,1)}, u32[]{:S(2)}, u32[]{:S(2)}) async-start(bf16[128,32,128]{2,0,1:T(8,128)(2,1)} %tile.11), calls=%async_computation.1 | async-start | bytes 2097152 | tf_op jit(solution)/shard_map/all_to_all | solution.py:15
  48.8 17.3 %all-to-all-done.1 = bf16[128,32,128]{2,0,1:T(8,128)(2,1)} async-done(((bf16[128,32,128]{2,0,1:T(8,128)(2,1)}), bf16[128,32,128]{2,0,1:T(8,128)(2,1)}, u32[]{:S(2)}, u32[]{:S(2)}) %all-to-all-start.1) | async-done | bytes 1048608 | tf_op jit(solution)/shard_map/all_to_all | solution.py:15
  69.5 3.5 collective-permute-done.1
  75.0 5.8 %all-to-all-start.2 = ((bf16[128,32,128]{2,0,1:T(8,128)(2,1)}), bf16[128,32,128]{2,0,1:T(8,128)(2,1)}, u32[]{:S(2)}, u32[]{:S(2)}) async-start(bf16[128,32,128]{2,0,1:T(8,128)(2,1)} %tile.12), calls=%async_computation.2 | async-start | bytes 2097152 | tf_op jit(solution)/shard_map/all_to_all | solution.py:15
  80.8 17.3 %all-to-all-done.2 = bf16[128,32,128]{2,0,1:T(8,128)(2,1)} async-done(((bf16[128,32,128]{2,0,1:T(8,128)(2,1)}), bf16[128,32,128]{2,0,1:T(8,128)(2,1)}, u32[]{:S(2)}, u32[]{:S(2)}) %all-to-all-start.2) | async-done | bytes 1048608 | tf_op jit(solution)/shard_map/all_to_all | solution.py:15
  98.1 2.3 copy.9
  103.4 3.5 collective-permute-done.2
  108.8 5.8 %all-to-all-start.3 = ((bf16[128,32,128]{2,0,1:T(8,128)(2,1)}), bf16[128,32,128]{2,0,1:T(8,128)(2,1)}, u32[]{:S(2)}, u32[]{:S(2)}) async-start(bf16[128,32,128]{2,0,1:T(8,128)(2,1)} %tile.13), calls=%async_computation.3 | async-start | bytes 2097152 | tf_op jit(solution)/shard_map/all_to_all | solution.py:15
  114.7 17.3 %all-to-all-done.3 = bf16[128,32,128]{2,0,1:T(8,128)(2,1)} async-done(((bf16[128,32,128]{2,0,1:T(8,128)(2,1)}), bf16[128,32,128]{2,0,1:T(8,128)(2,1)}, u32[]{:S(2)}, u32[]{:S(2)}) %all-to-all-start.3) | async-done | bytes 1048608 | tf_op jit(solution)/shard_map/all_to_all | solution.py:15
  132.0 2.3 copy.10
  137.3 3.5 collective-permute-done.3
  142.8 5.8 %all-to-all-start.4 = ((bf16[128,32,128]{2,0,1:T(8,128)(2,1)}), bf16[128,32,128]{2,0,1:T(8,128)(2,1)}, u32[]{:S(2)}, u32[]{:S(2)}) async-start(bf16[128,32,128]{2,0,1:T(8,128)(2,1)} %tile.14), calls=%async_computation.4 | async-start | bytes 2097152 | tf_op jit(solution)/shard_map/all_to_all | solution.py:15
  148.7 1.8 convolution_select_fusion.3
  152.3 1.8 convolution_select_fusion.1
  154.1 11.9 %all-to-all-done.4 = bf16[128,32,128]{2,0,1:T(8,128)(2,1)} async-done(((bf16[128,32,128]{2,0,1:T(8,128)(2,1)}), bf16[128,32,128]{2,0,1:T(8,128)(2,1)}, u32[]{:S(2)}, u32[]{:S(2)}) %all-to-all-start.4) | async-done | bytes 1048608 | tf_op jit(solution)/shard_map/all_to_all | solution.py:15
  169.4 4.9 %fusion.10 = (f32[]{:T(128)}, bf16[128,4096]{1,0:T(8,128)(2,1)}) fusion(f32[128,4096]{1,0:T(8,128)S(1)} %convolution_select_fusion, f32[128,4096]{1,0:T(8,128)} %convolution_select_fusion.1, f32[128,4096]{1,0:T(8,128)} %convolution_select_fusion.2, f32[128,4096]{1,0:T(8,128)S(1)} %copy-done.4, bf16[128,4096]{0,1:T(8,128)(2,1)S(1)} %bitcast.130, ...), kind=kOutput, calls=%fused_computation.21 | convolution fusion | flops 140509184 | bytes 11567113 | tf_op jit(solution)/shard_map/dot_general | solution.py:60
  174.4 63.2 %psum.7 = f32[]{:T(128)} all-reduce(f32[]{:T(128)} %get-tuple-element.13), channel_id=1, replica_groups=mesh['pipe'=4,'dp'=32] {'dp'}, use_global_device_ids=true, to_apply=%region_1.2 | all-reduce | flops 1 | bytes 8 | tf_op jit(solution)/shard_map/psum | solution.py:69
  238.3 2.4 fusion.11
  241.2 112.3 %all-gather.2.cloned.1.call-done = bf16[4096,4096]{1,0:T(8,128)(2,1)} async-done(((bf16[128,4096]{1,0:T(8,128)(2,1)}), bf16[4096,4096]{1,0:T(8,128)(2,1)}) %all-gather.2.cloned.1.call-update) | async-done | bytes 33554448 | tf_op jit(solution)/shard_map/all_gather | solution.py:72
  353.5 31.4 %convolution_convert_fusion.1 = bf16[128,4096]{1,0:T(8,128)(2,1)S(1)} fusion(bf16[4096,4096]{1,0:T(8,128)(2,1)} %all-gather.2.cloned.1.call-done, bf16[128,4096]{1,0:T(8,128)(2,1)S(1)} %copy-done.1), kind=kOutput, calls=%fused_computation.15 | convolution fusion | flops 8590983168 | bytes 35651584 | tf_op jit(solution)/shard_map/dot_general | solution.py:74
  384.9 32.8 %fusion.9 = bf16[1,128,4096]{2,1,0:T(8,128)(2,1)} fusion(bf16[4096,4096]{1,0:T(8,128)(2,1)} %all-gather.2.cloned.1.call-done, bf16[128,4096]{1,0:T(8,128)(2,1)S(1)} %convolution_convert_fusion.1, bf16[128,4096]{1,0:T(8,128)(2,1)S(1)} %copy-done.1), kind=kOutput, calls=%fused_computation.18 | convolution fusion | flops 8595177472 | bytes 36700160 | tf_op jit(solution)/shard_map/dot_general | solution.py:78
  (47 shorter events, 27.1 us)
Async XLA Ops:
  7.2 29.4 %copy-start = (bf16[1,128,4096]{2,1,0:T(8,128)(2,1)S(1)}, bf16[1,128,4096]{2,1,0:T(8,128)(2,1)}, u32[]{:S(2)}) copy-start(bf16[1,128,4096]{2,1,0:T(8,128)(2,1)} %param.6) | copy-start | bytes 3145732
  7.2 11.5 %copy-start.8 = (bf16[1,2,128,128]{3,2,1,0:T(8,128)(2,1)S(1)}, bf16[1,2,128,128]{3,2,1,0:T(8,128)(2,1)}, u32[]{:S(2)}) copy-start(bf16[1,2,128,128]{3,2,1,0:T(8,128)(2,1)} %param.5) | copy-start | bytes 196612
  9.3 26.6 %all-to-all-start = ((bf16[128,32,128]{2,0,1:T(8,128)(2,1)}), bf16[128,32,128]{2,0,1:T(8,128)(2,1)S(1)}, u32[]{:S(2)}, u32[]{:S(2)}) async-start(bf16[128,32,128]{2,0,1:T(8,128)(2,1)} %tile.10), calls=%async_computation | async-start | bytes 2097152 | tf_op jit(solution)/shard_map/all_to_all | solution.py:15
  18.8 22.9 %copy-start.6 = (bf16[2,128,128]{2,1,0:T(8,128)(2,1)S(1)}, bf16[2,128,128]{2,1,0:T(8,128)(2,1)}, u32[]{:S(2)}) copy-start(bf16[2,128,128]{2,1,0:T(8,128)(2,1)} %param.4) | copy-start | bytes 196612
  37.1 4.7 %collective-permute-start = (bf16[128,128]{1,0:T(8,128)(2,1)S(1)}, bf16[128,128]{1,0:T(8,128)(2,1)S(1)}, u32[]{:S(2)}, u32[]{:S(2)}) collective-permute-start(bf16[128,128]{1,0:T(8,128)(2,1)S(1)} %get-tuple-element.6), channel_id=1, source_target_pairs={{32,0},{64,32},{96,64},{33,1},{65,33},{97,65},{34,2},{66,34},{98,6... | collective-permute-start | bytes 98312 | tf_op jit(solution)/shard_map/ppermute | solution.py:21
  43.0 23.1 %all-to-all-start.1 = ((bf16[128,32,128]{2,0,1:T(8,128)(2,1)}), bf16[128,32,128]{2,0,1:T(8,128)(2,1)}, u32[]{:S(2)}, u32[]{:S(2)}) async-start(bf16[128,32,128]{2,0,1:T(8,128)(2,1)} %tile.11), calls=%async_computation.1 | async-start | bytes 2097152 | tf_op jit(solution)/shard_map/all_to_all | solution.py:15
  68.2 4.8 %collective-permute-start.1 = (bf16[128,128]{1,0:T(8,128)(2,1)S(1)}, bf16[128,128]{1,0:T(8,128)(2,1)}, u32[]{:S(2)}, u32[]{:S(2)}) collective-permute-start(bf16[128,128]{1,0:T(8,128)(2,1)S(1)} %get-tuple-element.8), channel_id=1, source_target_pairs={{32,0},{64,32},{96,64},{33,1},{65,33},{97,65},{34,2},{66,34},{98,6... | collective-permute-start | bytes 98312 | tf_op jit(solution)/shard_map/ppermute | solution.py:21
  75.0 23.1 %all-to-all-start.2 = ((bf16[128,32,128]{2,0,1:T(8,128)(2,1)}), bf16[128,32,128]{2,0,1:T(8,128)(2,1)}, u32[]{:S(2)}, u32[]{:S(2)}) async-start(bf16[128,32,128]{2,0,1:T(8,128)(2,1)} %tile.12), calls=%async_computation.2 | async-start | bytes 2097152 | tf_op jit(solution)/shard_map/all_to_all | solution.py:15
  102.1 4.8 %collective-permute-start.2 = (bf16[128,128]{1,0:T(8,128)(2,1)S(1)}, bf16[128,128]{1,0:T(8,128)(2,1)}, u32[]{:S(2)}, u32[]{:S(2)}) collective-permute-start(bf16[128,128]{1,0:T(8,128)(2,1)S(1)} %get-tuple-element.10), channel_id=1, source_target_pairs={{32,0},{64,32},{96,64},{33,1},{65,33},{97,65},{34,2},{66,34},{98,6... | collective-permute-start | bytes 98312 | tf_op jit(solution)/shard_map/ppermute | solution.py:21
  108.8 23.1 %all-to-all-start.3 = ((bf16[128,32,128]{2,0,1:T(8,128)(2,1)}), bf16[128,32,128]{2,0,1:T(8,128)(2,1)}, u32[]{:S(2)}, u32[]{:S(2)}) async-start(bf16[128,32,128]{2,0,1:T(8,128)(2,1)} %tile.13), calls=%async_computation.3 | async-start | bytes 2097152 | tf_op jit(solution)/shard_map/all_to_all | solution.py:15
  136.0 4.8 %collective-permute-start.3 = (bf16[128,128]{1,0:T(8,128)(2,1)S(1)}, bf16[128,128]{1,0:T(8,128)(2,1)}, u32[]{:S(2)}, u32[]{:S(2)}) collective-permute-start(bf16[128,128]{1,0:T(8,128)(2,1)S(1)} %get-tuple-element.12), channel_id=1, source_target_pairs={{32,0},{64,32},{96,64},{33,1},{65,33},{97,65},{34,2},{66,34},{98,6... | collective-permute-start | bytes 98312 | tf_op jit(solution)/shard_map/ppermute | solution.py:21
  142.8 23.1 %all-to-all-start.4 = ((bf16[128,32,128]{2,0,1:T(8,128)(2,1)}), bf16[128,32,128]{2,0,1:T(8,128)(2,1)}, u32[]{:S(2)}, u32[]{:S(2)}) async-start(bf16[128,32,128]{2,0,1:T(8,128)(2,1)} %tile.14), calls=%async_computation.4 | async-start | bytes 2097152 | tf_op jit(solution)/shard_map/all_to_all | solution.py:15
  148.6 204.9 %all-gather.2.cloned.1.call-start = ((), (), s32[]{:S(2)}) async-start(), calls=%async_computation.5 | async-start | bytes 34603008 | tf_op jit(solution)/shard_map/all_gather | solution.py:72
  148.7 1.8 copy-start.2
  150.5 1.8 copy-start.3
  167.6 1.6 copy-start.4
  167.6 1.8 copy-start.5
  240.7 112.8 %copy-start.1 = (bf16[128,4096]{1,0:T(8,128)(2,1)S(1)}, bf16[128,4096]{1,0:T(8,128)(2,1)}, u32[]{:S(2)}) copy-start(bf16[128,4096]{1,0:T(8,128)(2,1)} %fusion.11) | copy-start | bytes 3145732
  241.2 143.7 %copy-start.7 = (bf16[1,2,128,128]{3,2,1,0:T(8,128)(2,1)}, bf16[1,2,128,128]{3,2,1,0:T(8,128)(2,1)S(1)}, u32[]{:S(2)}) copy-start(bf16[1,2,128,128]{3,2,1,0:T(8,128)(2,1)S(1)} %fusion.28) | copy-start | bytes 196612
Sparse Core Ops, SparseCore 0:
  240.8 112.6 all-gather.1
